TPU v7x, 32 devices: a whole 2x2x4 slice. The times are simulated.
32 devices in a mesh: grp: 4 (over y, x), dev: 8 (over z, core).
Axes of the slice: x: 2, y: 2, z: 4, core: 2. Of those that a mesh axis runs over, the one named last changes fastest.
Arguments:
- child_weights: float32 [2, 256, 4, 64, 64], P(None, ('grp', 'dev')), may hold values from -0.12 to 0.12
- pivots: int32 [256, 32], P(('grp', 'dev')), may hold values from 0 to 1023, as said below
- ranks: int32 [256], replicated, may hold values from 1 to 32, 2560 in all
- owner_slot: int32 [256], replicated, may hold values from 0 to 255, each once
Outputs:
- skeleton_sums: float32 [2, 32, 256, 64], P(None, None, ('grp', 'dev'))
Inputs may be any that keep to these rules, and one draw needn't show every extreme that they name: `pivots`: each row lists 32 distinct points of one target box, numbered row by row within the box. The ranks sum to 2560; some box has rank 32. A permutation: box a is owned by device floor(owner_slot[a] / 8) of grp+dev, at place owner_slot[a] mod 8.
All inputs are finite; a program needn't handle non-finite values.
Results may differ from a plain program's by a relative error of at most 0.0003.
Values sent between devices are 32-bit elements; how exact they have to be, the bound alone decides.
A program may use at most 64 MiB of HBM per device.

v0:
```python
import math

import jax
import jax.numpy as jnp
import numpy as np
from jax import lax
from jax.experimental import pallas as pl
from jax.experimental.pallas import tpu as pltpu
from jax.sharding import PartitionSpec as P

GRID = 2048
Q = 8
RT = 32
RMEAN = 10
SIDE = GRID // 32
WIDTH = GRID // 64
ROW = GRID // 64
COLS = GRID // 32
LANES = 128
R = Q * Q

SIN = (4.442867904603554, -7.30744348201647, 3.594788644821573, -0.7843755040132807)
COS = (1.414204082132758, -6.977642209183305, 5.715240371096478, -1.7283548501332477)

F32 = jnp.float32
BF16 = jnp.bfloat16
CONTRACT = (((1,), (1,)), ((), ()))


def nodes():
    return np.cos(np.pi * (2.0 * np.arange(Q) + 1.0) / (2.0 * Q))


def lagrange(at, points):
    out = np.ones((Q, Q))
    for t in range(Q):
        for k in range(Q):
            if k != t:
                out[t] *= (points - at[k]) / (at[t] - at[k])
    return out


def child_table():
    c = nodes()
    halves = np.stack([lagrange(c, u - 0.5 + 0.5 * c) for u in (0.0, 1.0)])
    return np.einsum("uaj,vbk->abuvjk", halves, halves).reshape(R, 4 * R)


def split_table():
    table = child_table().astype(np.float32)
    high = table.astype(jnp.bfloat16)
    low = (table - high.astype(np.float32)).astype(jnp.bfloat16)
    return np.concatenate([high, low, high], axis=1)


def offsets():
    c = nodes()
    parent = SIDE / 2 - 0.5 + SIDE / 2 * c
    child = np.concatenate([SIDE * u / 2 + SIDE / 4 - 0.5 + SIDE / 4 * c for u in (0, 1)])
    return child, parent


def centre_rows(targets):
    a = np.arange(targets)
    x1 = (2 * WIDTH * (a // COLS) + WIDTH - 1) / (2 * GRID)
    x2 = (2 * WIDTH * (a % COLS) + WIDTH - 1) / (2 * GRID)
    c1 = (2 + np.sin(16 * np.pi * x1) * np.sin(16 * np.pi * x2)) / 16
    c2 = (2 + np.cos(16 * np.pi * x1) * np.cos(16 * np.pi * x2)) / 16
    child, parent = offsets()
    rows = [np.stack([c1, c2] + [np.zeros(targets)] * 6)]
    for o in (child, parent):
        for x in (x1, x2):
            turn = o[:, None] * x[None, :]
            rows.append(turn - np.floor(turn))
    return np.concatenate(rows).astype(np.float32)


def offset_columns():
    child, parent = offsets()
    return np.broadcast_to(np.concatenate([child, parent])[:, None], (3 * Q, LANES)).astype(np.float32)


def half_turn(phase):
    r = phase - jnp.round(phase)
    q = r * r
    s = SIN[3]
    for coefficient in SIN[2::-1]:
        s = s * q + coefficient
    s = s * r
    c = COS[3]
    for coefficient in COS[2::-1]:
        c = c * q + coefficient
    return 1.0 - s * s, s * c


def root(square):
    return square * lax.rsqrt(square)


def corner(own_boxes, box):
    position = lax.axis_index("grp") * lax.axis_size("dev") + lax.axis_index("dev")
    box_id = position * own_boxes + box
    return (box_id // ROW) * SIDE - GRID // 2, (box_id % ROW) * SIDE - GRID // 2


def outer(column, tile):
    return jnp.concatenate([column[j : j + 1] + tile for j in range(Q)], axis=0)


def source_box(own_boxes, targets, parents, b, weights_ref, table_ref, centre_ref, offset_ref, delta_ref):
    k1, k2 = corner(own_boxes, b)
    k1f, k2f = k1.astype(F32), k2.astype(F32)
    offs = offset_ref[...]
    for g in range(targets // LANES):
        lanes = slice(g * LANES, (g + 1) * LANES)
        lane = lax.broadcasted_iota(jnp.int32, (1, LANES), 1)
        box = lane + g * LANES
        h1 = 2 * WIDTH * (box // COLS) + WIDTH - 1
        h2 = 2 * WIDTH * (box % COLS) + WIDTH - 1
        whole = ((h1 * k1 + h2 * k2) & (2 * GRID - 1)).astype(F32) * (1.0 / (2 * GRID))
        c1 = centre_ref[0:1, lanes]
        c2 = centre_ref[1:2, lanes]
        first = c1 * (k1f + offs)
        first = first * first
        second = c2 * (k2f + offs)
        second = second * second
        turn1 = centre_ref[8 : 8 + 2 * Q, lanes]
        turn2 = centre_ref[8 + 2 * Q : 8 + 4 * Q, lanes] + whole
        back1 = centre_ref[8 + 4 * Q : 8 + 5 * Q, lanes]
        back2 = centre_ref[8 + 5 * Q : 8 + 6 * Q, lanes] + whole
        parent_lane = (g * (COLS // 2)) % LANES + (lane % COLS) // 2
        pick = jnp.broadcast_to(parent_lane, (R, LANES))
        start = (g * (COLS // 2)) // LANES * LANES
        high, low = [], []
        for u in range(2):
            for v in range(2):
                one, two = slice(u * Q, (u + 1) * Q), slice(v * Q, (v + 1) * Q)
                phase = root(outer(first[one], second[two])) + outer(turn1[one], turn2[two])
                cosine, sine = half_turn(phase)
                spread = []
                for z in range(2):
                    w = weights_ref[z, b, 2 * u + v, :, start : min(start + LANES, parents)]
                    if w.shape[1] < LANES:
                        w = jnp.concatenate([w] * (LANES // w.shape[1]), axis=1)
                    spread.append(jnp.take_along_axis(w, pick, axis=1, mode="promise_in_bounds"))
                wr, wi = spread
                both = jnp.concatenate([wr * cosine + wi * sine, wi * cosine - wr * sine], axis=1)
                top = both.astype(BF16)
                high.append(top)
                low.append((both - top.astype(F32)).astype(BF16))
        moved = jnp.concatenate(high + high + low, axis=0)
        interp = jnp.dot(table_ref[...], moved, preferred_element_type=F32)
        ir, ii = interp[:, :LANES], interp[:, LANES:]
        parent = slice(2 * Q, 3 * Q)
        phase = root(outer(first[parent], second[parent])) + outer(back1, back2)
        cosine, sine = half_turn(phase)
        for z, part in enumerate((ir * cosine - ii * sine, ii * cosine + ir * sine)):
            top = part.astype(BF16)
            delta_ref[b, z * R : (z + 1) * R, lanes] = top
            delta_ref[b, z * R : (z + 1) * R, targets + g * LANES : targets + (g + 1) * LANES] = (
                part - top.astype(F32)
            ).astype(BF16)


def row_facts(targets, c, span, facts, firsts, ends):
    row = lax.broadcasted_iota(jnp.int32, (span, targets), 0) + c * span
    hot = jnp.where((firsts <= row) & (row < ends), 1.0, 0.0).astype(BF16)
    here = lax.dot_general(facts, hot, CONTRACT, preferred_element_type=F32).astype(jnp.int32)
    place = lax.broadcasted_iota(jnp.int32, (1, span), 1) + c * span
    rank = place - (here[2 * RT + 2 : 2 * RT + 3] * LANES + here[2 * RT + 3 : 2 * RT + 4])
    mine = lax.broadcasted_iota(jnp.int32, (RT, span), 0) == rank
    p1 = jnp.sum(jnp.where(mine, here[:RT], 0), axis=0, keepdims=True)
    p2 = jnp.sum(jnp.where(mine, here[RT : 2 * RT], 0), axis=0, keepdims=True)
    h1 = here[2 * RT : 2 * RT + 1] * WIDTH + p1
    h2 = here[2 * RT + 1 : 2 * RT + 2] * WIDTH + p2
    points = jnp.concatenate([h1, h2], axis=0)
    angle = ((8 * points) & (GRID - 1)).astype(F32) * (2.0 * math.pi / GRID)
    sines, cosines = jnp.sin(angle), jnp.cos(angle)
    c1 = (2.0 + sines[0:1] * sines[1:2]) * (1.0 / 16)
    c2 = (2.0 + cosines[0:1] * cosines[1:2]) * (1.0 / 16)
    return hot, jnp.concatenate([points.astype(F32), c1, c2], axis=0)


def skeleton_rows(own_boxes, boxes, span, hot, point, delta_ref, offs):
    twice = jnp.concatenate([hot, hot], axis=1)
    h1, h2 = point[0:1].astype(jnp.int32), point[1:2].astype(jnp.int32)
    c1, c2 = point[2:3], point[3:4]
    turn1 = point[0:1] * (1.0 / GRID) * offs
    turn1 = turn1 - jnp.floor(turn1)
    turn2 = point[1:2] * (1.0 / GRID) * offs
    turn2 = turn2 - jnp.floor(turn2)
    first = c1 * (corner(own_boxes, 0)[0].astype(F32) + offs)
    first = first * first
    sums = []
    for b in boxes:
        k1, k2 = corner(own_boxes, b)
        picked = lax.dot_general(delta_ref[b], twice, CONTRACT, preferred_element_type=F32)
        wr, wi = picked[:R], picked[R:]
        whole = ((h1 * k1 + h2 * k2) & (GRID - 1)).astype(F32) * (1.0 / GRID)
        second = c2 * (k2.astype(F32) + offs)
        second = second * second
        phase = root(outer(first, second)) + outer(turn1, turn2 + whole)
        cosine, sine = half_turn(phase)
        real = wr * cosine - wi * sine
        imag = wr * sine + wi * cosine
        sums.append((jnp.sum(real.reshape(Q, Q, span), axis=0), jnp.sum(imag.reshape(Q, Q, span), axis=0)))
    return jnp.concatenate(
        [
            jnp.sum(sums[n][z] + sums[n + 1][z], axis=0, keepdims=True)
            for z in range(2)
            for n in range(0, len(boxes), 2)
        ],
        axis=0,
    )


def kernel(
    own_boxes, targets, parents, devices, depth,
    weights_hbm, pivots_hbm, ranks_hbm, owner_hbm, table_hbm, centre_hbm, offset_hbm, out_ref,
    weights, table, centre, offset, ranks_row, owner_row, all_pivots, delta, begin_row, begin,
    hots, points, compact, places, rows,
    weights_sem, const_sem, begin_sem, pivot_send, pivot_recv, rows_send, rows_recv,
):
    me = lax.axis_index("grp") * depth + lax.axis_index("dev")
    span = 2 * LANES
    spans = targets * RMEAN // span

    def device(index):
        return (index // depth, index % depth)

    barrier = pltpu.get_barrier_semaphore()

    def greet(j, carry):
        pl.semaphore_signal(
            barrier, inc=1, device_id=device(lax.rem(me + j, devices)), device_id_type=pl.DeviceIdType.MESH
        )
        return carry

    pairs = [
        (ranks_hbm, ranks_row),
        (owner_hbm, owner_row),
        (table_hbm, table),
        (centre_hbm, centre),
        (offset_hbm, offset),
        (pivots_hbm, all_pivots.at[me]),
    ]
    consts = [pltpu.make_async_copy(far, near, const_sem.at[n]) for n, (far, near) in enumerate(pairs)]
    loads = [
        pltpu.make_async_copy(weights_hbm.at[:, b], weights.at[:, b], weights_sem.at[b]) for b in range(own_boxes)
    ]
    for copy in consts + loads:
        copy.start()
    lax.fori_loop(1, devices, greet, 0)
    for copy in consts:
        copy.wait()

    ranks = ranks_row[...]
    owners = owner_row[...]
    rank_down = jnp.broadcast_to(ranks, (targets, targets)).T
    owner_down = jnp.broadcast_to(owners, (targets, targets)).T
    slots = lax.broadcasted_iota(jnp.int32, (1, targets), 1)
    firsts = jnp.sum(jnp.where(owner_down < owners, rank_down, 0), axis=0, keepdims=True)
    ends = firsts + ranks
    begins = jnp.sum(jnp.where(owner_down < slots, rank_down, 0), axis=0, keepdims=True)
    begin_row[:, :targets] = begins
    begin_row[:, targets:] = jnp.full((1, LANES), targets * RMEAN, jnp.int32)
    to_scalars = pltpu.make_async_copy(begin_row, begin, begin_sem)
    to_scalars.start()

    def pivot_copy(target, source):
        return pltpu.make_async_remote_copy(
            src_ref=pivots_hbm,
            dst_ref=all_pivots.at[source],
            send_sem=pivot_send.at[target],
            recv_sem=pivot_recv.at[source],
            device_id=device(target),
            device_id_type=pl.DeviceIdType.MESH,
        )

    def send_pivots(j, carry):
        pivot_copy(lax.rem(me + j, devices), me).start()
        return carry

    def one_box(b, carry):
        pltpu.make_async_copy(weights_hbm.at[:, b], weights.at[:, b], weights_sem.at[b]).wait()
        source_box(own_boxes, targets, parents, b, weights, table, centre, offset, delta)
        return carry

    lax.fori_loop(0, 2, one_box, 0)
    pl.semaphore_wait(barrier, devices - 1)
    lax.fori_loop(1, devices, send_pivots, 0)
    lax.fori_loop(2, own_boxes, one_box, 0)

    to_scalars.wait()
    boxes = LANES // RT
    groups = targets // devices // boxes
    tall = own_boxes // 2
    lane = lax.broadcasted_iota(jnp.int32, (tall, LANES), 1)

    def chunk_of(slot):
        return jnp.minimum(jnp.maximum(begin[0, slot], 0) // LANES, 2 * spans - 1)

    def one_place(owner, carry):
        parts = []
        for n in range(groups):
            slot = (owner * groups + n) * boxes
            edges = [begin[0, slot + k] for k in range(boxes + 1)]
            low = jnp.full((tall, LANES), edges[0], jnp.int32)
            high = jnp.full((tall, LANES), edges[1], jnp.int32)
            for k in range(1, boxes):
                low = jnp.where(lane >= k * RT, edges[k], low)
                high = jnp.where(lane >= k * RT, edges[k + 1], high)
            index = low + (lane & (RT - 1))
            parts.append(jnp.where(index < high, index - chunk_of(slot) * LANES, -1))
        places[owner] = jnp.concatenate(parts, axis=0)
        return carry

    lax.fori_loop(0, devices, one_place, 0)

    def wait_pivots(j, carry):
        other = lax.rem(me + j, devices)
        copy = pivot_copy(other, other)
        copy.wait_send()
        copy.wait_recv()
        return carry

    lax.fori_loop(1, devices, wait_pivots, 0)
    columns = all_pivots[...].reshape(targets, RT).astype(F32).T.astype(jnp.int32)
    facts = jnp.concatenate(
        [columns // WIDTH, columns % WIDTH, slots // COLS, slots % COLS, firsts // LANES, firsts % LANES]
        + [jnp.zeros((12, targets), jnp.int32)],
        axis=0,
    )
    facts = facts.astype(F32).astype(BF16)
    offs = offset[2 * Q : 3 * Q]
    offs = jnp.concatenate([offs, offs], axis=1)

    def one_fact(c, carry):
        hot, point = row_facts(targets, c, span, facts, firsts, ends)
        hots[c] = hot
        points[c, 0:4] = point
        return carry

    lax.fori_loop(0, spans, one_fact, 0)
    compact[2 * spans] = jnp.zeros((tall * groups, LANES), F32)

    def rows_copy(half, target, source):
        return pltpu.make_async_remote_copy(
            src_ref=rows.at[half, target],
            dst_ref=out_ref.at[half, source],
            send_sem=rows_send.at[half, target],
            recv_sem=rows_recv.at[half, source],
            device_id=device(target),
            device_id_type=pl.DeviceIdType.MESH,
        )

    for half in range(2):
        mine = range(half * own_boxes // 2, (half + 1) * own_boxes // 2)

        def one_span(c, carry):
            block = skeleton_rows(own_boxes, mine, span, hots[c], points[c], delta, offs)
            block = jnp.concatenate([block] * groups, axis=0)
            compact[2 * c] = block[:, :LANES]
            compact[2 * c + 1] = block[:, LANES:]
            return carry

        def place_rows(owner):
            chunks = [chunk_of((owner * groups + n) * boxes) for n in range(groups)]
            near = jnp.concatenate(
                [compact[chunk][n * tall : (n + 1) * tall] for n, chunk in enumerate(chunks)], axis=0
            )
            far = jnp.concatenate(
                [compact[chunk + 1][n * tall : (n + 1) * tall] for n, chunk in enumerate(chunks)], axis=0
            )
            place = places[owner]
            within = place & (LANES - 1)
            near = jnp.take_along_axis(near, within, axis=1, mode="promise_in_bounds")
            far = jnp.take_along_axis(far, within, axis=1, mode="promise_in_bounds")
            return jnp.where(place < 0, 0.0, jnp.where(place >= LANES, far, near))

        def send_rows(j, carry):
            other = lax.rem(me + j, devices)
            rows[half, other] = place_rows(other)
            rows_copy(half, other, me).start()
            return carry

        lax.fori_loop(0, spans, one_span, 0)
        lax.fori_loop(1, devices, send_rows, 0)
        out_ref[half, me] = place_rows(me)

    def wait_rows(j, carry):
        other = lax.rem(me + j, devices)
        for half in range(2):
            copy = rows_copy(half, other, other)
            copy.wait_send()
            copy.wait_recv()
        return carry

    lax.fori_loop(1, devices, wait_rows, 0)


def local(child_weights, pivots, ranks, owner_slot):
    depth = lax.axis_size("dev")
    devices = lax.axis_size("grp") * depth
    own_boxes = child_weights.shape[1]
    parents = child_weights.shape[4]
    targets = ranks.shape[0]
    groups = targets // devices * RT // LANES
    tall = own_boxes // 2 * groups
    spans = targets * RMEAN // (2 * LANES)
    anywhere = pl.BlockSpec(memory_space=pl.ANY)
    table, centre, offs = split_table(), centre_rows(targets), offset_columns()
    dma = pltpu.SemaphoreType.DMA
    received = pl.pallas_call(
        lambda *refs: kernel(own_boxes, targets, parents, devices, depth, *refs),
        in_specs=[anywhere] * 7,
        out_specs=pl.BlockSpec(memory_space=pltpu.VMEM),
        out_shape=jax.ShapeDtypeStruct((2, devices, tall, LANES), F32),
        scratch_shapes=[
            pltpu.VMEM(child_weights.shape, F32),
            pltpu.VMEM(table.shape, BF16),
            pltpu.VMEM(centre.shape, F32),
            pltpu.VMEM(offs.shape, F32),
            pltpu.VMEM((1, targets), jnp.int32),
            pltpu.VMEM((1, targets), jnp.int32),
            pltpu.VMEM((devices,) + pivots.shape, jnp.int32),
            pltpu.VMEM((own_boxes, 2 * R, 2 * targets), BF16),
            pltpu.VMEM((1, targets + LANES), jnp.int32),
            pltpu.SMEM((1, targets + LANES), jnp.int32),
            pltpu.VMEM((spans, 2 * LANES, targets), BF16),
            pltpu.VMEM((spans, 8, 2 * LANES), F32),
            pltpu.VMEM((2 * spans + 1, tall, LANES), F32),
            pltpu.VMEM((devices, tall, LANES), jnp.int32),
            pltpu.VMEM((2, devices, tall, LANES), F32),
            dma((own_boxes,)),
            dma((6,)),
            dma,
            dma((devices,)),
            dma((devices,)),
            dma((2, devices)),
            dma((2, devices)),
        ],
        compiler_params=pltpu.CompilerParams(
            collective_id=0, has_side_effects=True, vmem_limit_bytes=60 << 20
        ),
    )(child_weights, pivots, ranks.reshape(1, targets), owner_slot.reshape(1, targets), table, centre, offs)

    quarter = own_boxes // 4
    pair = ROW // own_boxes
    received = received.reshape(2, devices // (2 * pair), 2, pair, groups, 2, quarter, LANES // RT, RT)
    summed = received[:, :, 0] + received[:, :, 1]
    result = jnp.transpose(summed, (4, 7, 3, 6, 1, 2, 0, 5))
    return result.reshape(2, RT, targets // devices, devices * own_boxes // 4)


def solution(mesh):
    in_specs = (P(None, ("grp", "dev"), None, None, None), P(("grp", "dev"), None), P(), P())
    out_specs = P(None, None, ("grp", "dev"), None)
    return jax.shard_map(local, mesh=mesh, in_specs=in_specs, out_specs=out_specs, check_vma=False)
```

profile of v0, /device:TPU:0, one launch (start us, length us, event | category | flops | bytes accessed | tf_op | source)
XLA Modules:
  0.0 40.7 jit_solution(6944241897667620265)
XLA Ops:
  0.0 37.8 %shard_map.73 = f32[2,32,8,128]{3,2,1,0:T(8,128)} custom-call(f32[2,8,4,64,64]{4,3,2,1,0:T(8,128)} %refs_0_.1, s32[8,32]{1,0:T(8,128)} %refs_1_.1, s32[1,256]{1,0:T(1,128)} %bitcast.10, s32[1,256]{1,0:T(1,128)} %bitcast.11, bf16[64,768]{1,0:T(8,128)(2,1)} %constant.6.clone.refs_4_, f32[56,256]{1,0:T(8,128)} %constant.7.clone.refs_5_, ...), custom_call_target="tpu_custom_call" | custom-call | tf_op jit(solution)/shard_map/pallas_call | solution.py:414
  37.8 1.4 %reshape.15 = f32[2,4,2,4,2,2,2,4,32]{8,7,6,5,4,3,2,1,0:T(4,128)S(1)} reshape(f32[2,32,8,128]{3,2,1,0:T(8,128)} %shard_map.73) | data formatting | bytes 524288 | tf_op jit(solution)/shard_map/reshape | solution.py:450
  39.2 0.2 fusion
  39.4 0.4 %copy_add_fusion = f32[2,4,1,4,2,2,2,4,32]{8,6,0,3,1,7,4,5,2:T(2,128)S(1)} fusion(f32[2,4,1,4,2,2,2,4,32]{8,7,6,5,4,3,2,1,0:T(4,128)S(1)} %get-tuple-element.6, f32[2,4,1,4,2,2,2,4,32]{8,7,6,5,4,3,2,1,0:T(4,128)S(1)} %get-tuple-element.5), kind=kLoop, calls=%fused_computation | loop fusion | flops 32768 | bytes 393216 | tf_op jit(solution)/shard_map/add | solution.py:451
  39.8 0.9 %copy.11 = f32[2,32,8,64]{3,2,1,0:T(8,128)} copy(f32[2,32,8,64]{1,3,2,0:T(8,128)S(1)} %bitcast.9) | data formatting | bytes 262144 | tf_op jit(solution)/shard_map/reshape | solution.py:453
where the time goes:
time: 40.9 us; the launch traced here: 40.7 us
  Pallas kernels  37.8 us (92%)
  local copies, waits for them, and re-layouts  2.46 us (6%)
  other arithmetic  0.41 us (1%)
    pallas_call x1, Pallas kernels, local(): pl.pallas_call(lambda *refs: kernel(own_boxes, targets, parents, devices,...  37.8 us
    reshape x1, local copies, waits for them, and re-layouts, local(): received.reshape(2, devices // (2 * pair), 2, pair, groups, 2, quarter, L...  1.39 us
    reshape x1, local copies, waits for them, and re-layouts, local(): return result.reshape(2, RT, targets // devices, devices * own_boxes // 4)  0.9 us

commit v1 on v0

--- a/solution.py
+++ b/solution.py
@@ -21,6 +21,8 @@
 
 SIN = (4.442867904603554, -7.30744348201647, 3.594788644821573, -0.7843755040132807)
 COS = (1.414204082132758, -6.977642209183305, 5.715240371096478, -1.7283548501332477)
+FINE_SIN = (4.442882938082702, -7.308249478180419, 3.6064755519164122, -0.8474705853915653, 0.1160367907993074, -0.009939639006380334)
+FINE_COS = (1.4142135623720344, -6.97886419922267, 5.739885708281956, -1.8883460761614363, 0.3328004285822709, -0.03645323263485946, 0.002602159860467781)
 
 F32 = jnp.float32
 BF16 = jnp.bfloat16
@@ -91,6 +93,17 @@
     for coefficient in COS[2::-1]:
         c = c * q + coefficient
     return 1.0 - s * s, s * c
+
+
+def exact_turn(r):
+    q = r * r
+    s, c = FINE_SIN[-1], FINE_COS[-1]
+    for coefficient in FINE_SIN[-2::-1]:
+        s = s * q + coefficient
+    for coefficient in FINE_COS[-2::-1]:
+        c = c * q + coefficient
+    s = s * r
+    return jnp.where(s * s < 1.0, 1.0 - s * s, c * c - 1.0), s * c
 
 
 def root(square):
@@ -174,8 +187,8 @@
     h1 = here[2 * RT : 2 * RT + 1] * WIDTH + p1
     h2 = here[2 * RT + 1 : 2 * RT + 2] * WIDTH + p2
     points = jnp.concatenate([h1, h2], axis=0)
-    angle = ((8 * points) & (GRID - 1)).astype(F32) * (2.0 * math.pi / GRID)
-    sines, cosines = jnp.sin(angle), jnp.cos(angle)
+    angle = ((8 * points) & (GRID - 1)).astype(F32) * (1.0 / GRID)
+    cosines, sines = exact_turn(angle - jnp.where(angle > 0.5, 1.0, 0.0))
     c1 = (2.0 + sines[0:1] * sines[1:2]) * (1.0 / 16)
     c2 = (2.0 + cosines[0:1] * cosines[1:2]) * (1.0 / 16)
     return hot, jnp.concatenate([points.astype(F32), c1, c2], axis=0)
@@ -217,7 +230,7 @@
 def kernel(
     own_boxes, targets, parents, devices, depth,
     weights_hbm, pivots_hbm, ranks_hbm, owner_hbm, table_hbm, centre_hbm, offset_hbm, out_ref,
-    weights, table, centre, offset, ranks_row, owner_row, all_pivots, delta, begin_row, begin,
+    weights, table, centre, offset, ranks_row, owner_row, all_pivots, delta, begin_row, stop_row, chunk_row, chunks,
     hots, points, compact, places, rows,
     weights_sem, const_sem, begin_sem, pivot_send, pivot_recv, rows_send, rows_recv,
 ):
@@ -226,7 +239,7 @@
     spans = targets * RMEAN // span
 
     def device(index):
-        return (index // depth, index % depth)
+        return (lax.div(index, depth), lax.rem(index, depth))
 
     barrier = pltpu.get_barrier_semaphore()
 
@@ -262,17 +275,18 @@
     firsts = jnp.sum(jnp.where(owner_down < owners, rank_down, 0), axis=0, keepdims=True)
     ends = firsts + ranks
     begins = jnp.sum(jnp.where(owner_down < slots, rank_down, 0), axis=0, keepdims=True)
-    begin_row[:, :targets] = begins
-    begin_row[:, targets:] = jnp.full((1, LANES), targets * RMEAN, jnp.int32)
-    to_scalars = pltpu.make_async_copy(begin_row, begin, begin_sem)
+    begin_row[...] = begins
+    stop_row[...] = jnp.sum(jnp.where(owner_down <= slots, rank_down, 0), axis=0, keepdims=True)
+    chunk_row[...] = jnp.minimum(begins // LANES, 2 * spans - 1)
+    to_scalars = pltpu.make_async_copy(chunk_row, chunks, begin_sem)
     to_scalars.start()
 
     def pivot_copy(target, source):
         return pltpu.make_async_remote_copy(
             src_ref=pivots_hbm,
             dst_ref=all_pivots.at[source],
-            send_sem=pivot_send.at[target],
-            recv_sem=pivot_recv.at[source],
+            send_sem=pivot_send,
+            recv_sem=pivot_recv,
             device_id=device(target),
             device_id_type=pl.DeviceIdType.MESH,
         )
@@ -291,40 +305,45 @@
     lax.fori_loop(1, devices, send_pivots, 0)
     lax.fori_loop(2, own_boxes, one_box, 0)
 
-    to_scalars.wait()
     boxes = LANES // RT
     groups = targets // devices // boxes
     tall = own_boxes // 2
-    lane = lax.broadcasted_iota(jnp.int32, (tall, LANES), 1)
-
-    def chunk_of(slot):
-        return jnp.minimum(jnp.maximum(begin[0, slot], 0) // LANES, 2 * spans - 1)
-
-    def one_place(owner, carry):
-        parts = []
-        for n in range(groups):
-            slot = (owner * groups + n) * boxes
-            edges = [begin[0, slot + k] for k in range(boxes + 1)]
-            low = jnp.full((tall, LANES), edges[0], jnp.int32)
-            high = jnp.full((tall, LANES), edges[1], jnp.int32)
-            for k in range(1, boxes):
-                low = jnp.where(lane >= k * RT, edges[k], low)
-                high = jnp.where(lane >= k * RT, edges[k + 1], high)
+    down = lax.broadcasted_iota(jnp.int32, (tall * groups, LANES), 0)
+    lane = lax.broadcasted_iota(jnp.int32, (tall * groups, LANES), 1)
+    opening = (down // tall) * boxes
+    slot_here = opening + lane // RT
+    per_tile = LANES // (groups * boxes)
+
+    def one_tile(n, carry):
+        for m in range(per_tile):
+            spot = pl.ds(pl.multiple_of(n * LANES, LANES), LANES)
+            first = jnp.broadcast_to(begin_row[:, spot], lane.shape)
+            last = jnp.broadcast_to(stop_row[:, spot], lane.shape)
+            tile_slot = slot_here + m * groups * boxes
+            low = jnp.take_along_axis(first, tile_slot, axis=1, mode="promise_in_bounds")
+            high = jnp.take_along_axis(last, tile_slot, axis=1, mode="promise_in_bounds")
+            start = jnp.take_along_axis(first, opening + m * groups * boxes, axis=1, mode="promise_in_bounds")
             index = low + (lane & (RT - 1))
-            parts.append(jnp.where(index < high, index - chunk_of(slot) * LANES, -1))
-        places[owner] = jnp.concatenate(parts, axis=0)
+            places[n * per_tile + m] = jnp.where(index < high, index - (start & -LANES), -1)
         return carry
 
-    lax.fori_loop(0, devices, one_place, 0)
-
-    def wait_pivots(j, carry):
-        other = lax.rem(me + j, devices)
-        copy = pivot_copy(other, other)
+    lax.fori_loop(0, targets // LANES, one_tile, 0)
+    to_scalars.wait()
+
+    def drain(block, send, receive):
+        copy = pltpu.make_async_remote_copy(
+            src_ref=block,
+            dst_ref=block,
+            send_sem=send,
+            recv_sem=receive,
+            device_id=device(lax.rem(me + 1, devices)),
+            device_id_type=pl.DeviceIdType.MESH,
+        )
         copy.wait_send()
         copy.wait_recv()
-        return carry
-
-    lax.fori_loop(1, devices, wait_pivots, 0)
+
+    others = pl.ds(0, devices - 1)
+    drain(all_pivots.at[others], pivot_send, pivot_recv)
     columns = all_pivots[...].reshape(targets, RT).astype(F32).T.astype(jnp.int32)
     facts = jnp.concatenate(
         [columns // WIDTH, columns % WIDTH, slots // COLS, slots % COLS, firsts // LANES, firsts % LANES]
@@ -341,15 +360,15 @@
         points[c, 0:4] = point
         return carry
 
-    lax.fori_loop(0, spans, one_fact, 0)
+    lax.fori_loop(0, spans, one_fact, 0, unroll=5 if spans % 5 == 0 else 1)
     compact[2 * spans] = jnp.zeros((tall * groups, LANES), F32)
 
     def rows_copy(half, target, source):
         return pltpu.make_async_remote_copy(
             src_ref=rows.at[half, target],
             dst_ref=out_ref.at[half, source],
-            send_sem=rows_send.at[half, target],
-            recv_sem=rows_recv.at[half, source],
+            send_sem=rows_send,
+            recv_sem=rows_recv,
             device_id=device(target),
             device_id_type=pl.DeviceIdType.MESH,
         )
@@ -364,39 +383,30 @@
             compact[2 * c + 1] = block[:, LANES:]
             return carry
 
-        def place_rows(owner):
-            chunks = [chunk_of((owner * groups + n) * boxes) for n in range(groups)]
-            near = jnp.concatenate(
-                [compact[chunk][n * tall : (n + 1) * tall] for n, chunk in enumerate(chunks)], axis=0
-            )
-            far = jnp.concatenate(
-                [compact[chunk + 1][n * tall : (n + 1) * tall] for n, chunk in enumerate(chunks)], axis=0
-            )
+        def place_rows(owner, carry):
+            slot = owner * groups * boxes
+            near, far = compact[chunks[0, slot]], compact[chunks[0, slot] + 1]
+            for n in range(1, groups):
+                chunk = chunks[0, slot + n * boxes]
+                near = jnp.where(down >= n * tall, compact[chunk], near)
+                far = jnp.where(down >= n * tall, compact[chunk + 1], far)
             place = places[owner]
             within = place & (LANES - 1)
             near = jnp.take_along_axis(near, within, axis=1, mode="promise_in_bounds")
             far = jnp.take_along_axis(far, within, axis=1, mode="promise_in_bounds")
-            return jnp.where(place < 0, 0.0, jnp.where(place >= LANES, far, near))
+            rows[half, owner] = jnp.where(place < 0, 0.0, jnp.where(place >= LANES, far, near))
+            return carry
 
         def send_rows(j, carry):
-            other = lax.rem(me + j, devices)
-            rows[half, other] = place_rows(other)
-            rows_copy(half, other, me).start()
+            rows_copy(half, lax.rem(me + j, devices), me).start()
             return carry
 
         lax.fori_loop(0, spans, one_span, 0)
+        lax.fori_loop(0, devices, place_rows, 0, unroll=8)
         lax.fori_loop(1, devices, send_rows, 0)
-        out_ref[half, me] = place_rows(me)
-
-    def wait_rows(j, carry):
-        other = lax.rem(me + j, devices)
-        for half in range(2):
-            copy = rows_copy(half, other, other)
-            copy.wait_send()
-            copy.wait_recv()
-        return carry
-
-    lax.fori_loop(1, devices, wait_rows, 0)
+        out_ref[half, me] = rows[half, me]
+
+    drain(out_ref.at[:, others], rows_send, rows_recv)
 
 
 def local(child_weights, pivots, ranks, owner_slot):
@@ -425,8 +435,10 @@
             pltpu.VMEM((1, targets), jnp.int32),
             pltpu.VMEM((devices,) + pivots.shape, jnp.int32),
             pltpu.VMEM((own_boxes, 2 * R, 2 * targets), BF16),
-            pltpu.VMEM((1, targets + LANES), jnp.int32),
-            pltpu.SMEM((1, targets + LANES), jnp.int32),
+            pltpu.VMEM((1, targets), jnp.int32),
+            pltpu.VMEM((1, targets), jnp.int32),
+            pltpu.VMEM((1, targets), jnp.int32),
+            pltpu.SMEM((1, targets), jnp.int32),
             pltpu.VMEM((spans, 2 * LANES, targets), BF16),
             pltpu.VMEM((spans, 8, 2 * LANES), F32),
             pltpu.VMEM((2 * spans + 1, tall, LANES), F32),
@@ -435,10 +447,10 @@
             dma((own_boxes,)),
             dma((6,)),
             dma,
-            dma((devices,)),
-            dma((devices,)),
-            dma((2, devices)),
-            dma((2, devices)),
+            dma,
+            dma,
+            dma,
+            dma,
         ],
         compiler_params=pltpu.CompilerParams(
             collective_id=0, has_side_effects=True, vmem_limit_bytes=60 << 20

time: 40.9 us -> 35.2 us (0.86)
  Pallas kernels: 37.8 us -> 32.1 us
    pallas_call x1, Pallas kernels: 37.8 us -> 32.1 us  [local(): pl.pallas_call(lambda *refs: kernel(own_boxes, targets, parents, devices,...]
where the time goes in v1:
time: 35.2 us; the launch traced here: 35 us
  Pallas kernels  32.1 us (91%)
  local copies, waits for them, and re-layouts  2.46 us (7%)
  other arithmetic  0.41 us (1%)
    pallas_call x1, Pallas kernels, local(): pl.pallas_call(lambda *refs: kernel(own_boxes, targets, parents, devices,...  32.1 us
    reshape x1, local copies, waits for them, and re-layouts, local(): received.reshape(2, devices // (2 * pair), 2, pair, groups, 2, quarter, L...  1.39 us
    reshape x1, local copies, waits for them, and re-layouts, local(): return result.reshape(2, RT, targets // devices, devices * own_boxes // 4)  0.9 us

profile of v1, /device:TPU:0, one launch (start us, length us, event | category | flops | bytes accessed | tf_op | source)
XLA Modules:
  0.0 35.0 jit_solution(17809702034729513506)
XLA Ops:
  0.0 32.1 %shard_map.73 = f32[2,32,8,128]{3,2,1,0:T(8,128)} custom-call(f32[2,8,4,64,64]{4,3,2,1,0:T(8,128)} %refs_0_.1, s32[8,32]{1,0:T(8,128)} %refs_1_.1, s32[1,256]{1,0:T(1,128)} %bitcast.10, s32[1,256]{1,0:T(1,128)} %bitcast.11, bf16[64,768]{1,0:T(8,128)(2,1)} %constant.6.clone.refs_4_, f32[56,256]{1,0:T(8,128)} %constant.7.clone.refs_5_, ...), custom_call_target="tpu_custom_call" | custom-call | tf_op jit(solution)/shard_map/pallas_call | solution.py:424
  32.2 1.4 %reshape.15 = f32[2,4,2,4,2,2,2,4,32]{8,7,6,5,4,3,2,1,0:T(4,128)S(1)} reshape(f32[2,32,8,128]{3,2,1,0:T(8,128)} %shard_map.73) | data formatting | bytes 524288 | tf_op jit(solution)/shard_map/reshape | solution.py:462
  33.6 0.2 fusion
  33.7 0.4 %copy_add_fusion = f32[2,4,1,4,2,2,2,4,32]{8,6,0,3,1,7,4,5,2:T(2,128)S(1)} fusion(f32[2,4,1,4,2,2,2,4,32]{8,7,6,5,4,3,2,1,0:T(4,128)S(1)} %get-tuple-element.6, f32[2,4,1,4,2,2,2,4,32]{8,7,6,5,4,3,2,1,0:T(4,128)S(1)} %get-tuple-element.5), kind=kLoop, calls=%fused_computation | loop fusion | flops 32768 | bytes 393216 | tf_op jit(solution)/shard_map/add | solution.py:463
  34.1 0.9 %copy.11 = f32[2,32,8,64]{3,2,1,0:T(8,128)} copy(f32[2,32,8,64]{1,3,2,0:T(8,128)S(1)} %bitcast.9) | data formatting | bytes 262144 | tf_op jit(solution)/shard_map/reshape | solution.py:465

commit v2 on v1

--- a/solution.py
+++ b/solution.py
@@ -17,6 +17,7 @@
 ROW = GRID // 64
 COLS = GRID // 32
 LANES = 128
+WHOLE = 1.5 * 2**23
 R = Q * Q
 
 SIN = (4.442867904603554, -7.30744348201647, 3.594788644821573, -0.7843755040132807)
@@ -83,7 +84,7 @@
 
 
 def half_turn(phase):
-    r = phase - jnp.round(phase)
+    r = phase - ((phase + WHOLE) - WHOLE)
     q = r * r
     s = SIN[3]
     for coefficient in SIN[2::-1]:
@@ -231,7 +232,7 @@
     own_boxes, targets, parents, devices, depth,
     weights_hbm, pivots_hbm, ranks_hbm, owner_hbm, table_hbm, centre_hbm, offset_hbm, out_ref,
     weights, table, centre, offset, ranks_row, owner_row, all_pivots, delta, begin_row, stop_row, chunk_row, chunks,
-    hots, points, compact, places, rows,
+    hots, points, compact, places, rows, got, mixed,
     weights_sem, const_sem, begin_sem, pivot_send, pivot_recv, rows_send, rows_recv,
 ):
     me = lax.axis_index("grp") * depth + lax.axis_index("dev")
@@ -366,7 +367,7 @@
     def rows_copy(half, target, source):
         return pltpu.make_async_remote_copy(
             src_ref=rows.at[half, target],
-            dst_ref=out_ref.at[half, source],
+            dst_ref=got.at[half, source],
             send_sem=rows_send,
             recv_sem=rows_recv,
             device_id=device(target),
@@ -404,9 +405,31 @@
         lax.fori_loop(0, spans, one_span, 0)
         lax.fori_loop(0, devices, place_rows, 0, unroll=8)
         lax.fori_loop(1, devices, send_rows, 0)
-        out_ref[half, me] = rows[half, me]
-
-    drain(out_ref.at[:, others], rows_send, rows_recv)
+        got[half, me] = rows[half, me]
+
+    drain(got.at[:, others], rows_send, rows_recv)
+
+    pair = ROW // own_boxes
+    few = own_boxes // 4
+
+    def mix(n, carry):
+        sums = []
+        for k in (2 * n, 2 * n + 1):
+            upper = lax.div(k, pair) * 2 * pair + lax.rem(k, pair)
+            sums += [got[half, upper] + got[half, upper + pair] for half in range(2)]
+        for part in range(2 * groups):
+            lines = slice(part * few, (part + 1) * few)
+            mixed[part, pl.ds(pl.multiple_of(n * 4 * few, 4 * few), 4 * few)] = jnp.concatenate(
+                [block[lines] for block in sums], axis=0
+            )
+        return carry
+
+    lax.fori_loop(0, devices // 4, mix, 0, unroll=4)
+    for n in range(groups):
+        for z in range(2):
+            turned = mixed[2 * n + z].T
+            for k in range(boxes):
+                out_ref[z, :, n * boxes + k, :] = turned[k * RT : (k + 1) * RT]
 
 
 def local(child_weights, pivots, ranks, owner_slot):
@@ -417,15 +440,16 @@
     targets = ranks.shape[0]
     groups = targets // devices * RT // LANES
     tall = own_boxes // 2 * groups
+    sources = devices * own_boxes // 4
     spans = targets * RMEAN // (2 * LANES)
     anywhere = pl.BlockSpec(memory_space=pl.ANY)
     table, centre, offs = split_table(), centre_rows(targets), offset_columns()
     dma = pltpu.SemaphoreType.DMA
-    received = pl.pallas_call(
+    return pl.pallas_call(
         lambda *refs: kernel(own_boxes, targets, parents, devices, depth, *refs),
         in_specs=[anywhere] * 7,
         out_specs=pl.BlockSpec(memory_space=pltpu.VMEM),
-        out_shape=jax.ShapeDtypeStruct((2, devices, tall, LANES), F32),
+        out_shape=jax.ShapeDtypeStruct((2, RT, targets // devices, sources), F32),
         scratch_shapes=[
             pltpu.VMEM(child_weights.shape, F32),
             pltpu.VMEM(table.shape, BF16),
@@ -444,6 +468,8 @@
             pltpu.VMEM((2 * spans + 1, tall, LANES), F32),
             pltpu.VMEM((devices, tall, LANES), jnp.int32),
             pltpu.VMEM((2, devices, tall, LANES), F32),
+            pltpu.VMEM((2, devices, tall, LANES), F32),
+            pltpu.VMEM((2 * groups, sources, LANES), F32),
             dma((own_boxes,)),
             dma((6,)),
             dma,
@@ -457,13 +483,6 @@
         ),
     )(child_weights, pivots, ranks.reshape(1, targets), owner_slot.reshape(1, targets), table, centre, offs)
 
-    quarter = own_boxes // 4
-    pair = ROW // own_boxes
-    received = received.reshape(2, devices // (2 * pair), 2, pair, groups, 2, quarter, LANES // RT, RT)
-    summed = received[:, :, 0] + received[:, :, 1]
-    result = jnp.transpose(summed, (4, 7, 3, 6, 1, 2, 0, 5))
-    return result.reshape(2, RT, targets // devices, devices * own_boxes // 4)
-
 
 def solution(mesh):
     in_specs = (P(None, ("grp", "dev"), None, None, None), P(("grp", "dev"), None), P(), P())

time: 35.2 us -> 34.4 us (0.977)
  local copies, waits for them, and re-layouts: 2.46 us -> 1.67 us
  other arithmetic: 0.41 us -> 0 us
  Pallas kernels: 32.1 us -> 32.5 us
    reshape x2 -> x0, local copies, waits for them, and re-layouts: 2.29 us -> none  [the longest x1 1.39 us: local(): received.reshape(2, devices // (2 * pair), 2, pair, groups, 2, quarter, L...]
    unnamed x0 -> x1, local copies, waits for them, and re-layouts: none -> 1.67 us
    add x1 -> x0, other arithmetic: 0.41 us -> none  [local(): summed = received[:, :, 0] + received[:, :, 1]]
where the time goes in v2:
time: 34.4 us; the launch traced here: 34.2 us
  Pallas kernels  32.5 us (94%)
  local copies, waits for them, and re-layouts  1.67 us (5%)
    pallas_call x1, Pallas kernels, local(): pl.pallas_call(lambda *refs: kernel(own_boxes, targets, parents, devices,...  32.5 us
    unnamed x1, local copies, waits for them, and re-layouts  1.67 us

profile of v2, /device:TPU:0, one launch (start us, length us, event | category | flops | bytes accessed | tf_op | source)
XLA Modules:
  0.0 34.2 jit_solution(4556219126114287719)
XLA Ops:
  0.0 32.5 %shard_map.73 = f32[2,32,8,64]{3,2,1,0:T(8,128)} custom-call(f32[2,8,4,64,64]{4,3,2,1,0:T(8,128)} %refs_0_.1, s32[8,32]{1,0:T(8,128)} %refs_1_.1, s32[1,256]{1,0:T(1,128)} %bitcast.2, s32[1,256]{1,0:T(1,128)} %bitcast.3, bf16[64,768]{1,0:T(8,128)(2,1)} %constant.6.clone.refs_4_, f32[56,256]{1,0:T(8,128)} %constant.7.clone.refs_5_, ...), custom_call_target="tpu_custom_call" | custom-call | tf_op jit(solution)/shard_map/pallas_call | solution.py:448
  32.5 1.7 %copy.9 = f32[2,32,8,64]{3,2,1,0:T(8,128)} copy(f32[2,32,8,64]{3,2,1,0:T(8,128)} %shard_map.73) | data formatting | bytes 262144

commit v3 on v2

--- a/solution.py
+++ b/solution.py
@@ -53,7 +53,7 @@
     table = child_table().astype(np.float32)
     high = table.astype(jnp.bfloat16)
     low = (table - high.astype(np.float32)).astype(jnp.bfloat16)
-    return np.concatenate([high, low, high], axis=1)
+    return np.concatenate([high, low], axis=0)
 
 
 def offsets():
@@ -162,8 +162,9 @@
                 top = both.astype(BF16)
                 high.append(top)
                 low.append((both - top.astype(F32)).astype(BF16))
-        moved = jnp.concatenate(high + high + low, axis=0)
-        interp = jnp.dot(table_ref[...], moved, preferred_element_type=F32)
+        wide = jnp.dot(table_ref[...], jnp.concatenate(high, axis=0), preferred_element_type=F32)
+        fine = jnp.dot(table_ref[:R], jnp.concatenate(low, axis=0), preferred_element_type=F32)
+        interp = wide[:R] + (wide[R:] + fine)
         ir, ii = interp[:, :LANES], interp[:, LANES:]
         parent = slice(2 * Q, 3 * Q)
         phase = root(outer(first[parent], second[parent])) + outer(back1, back2)
@@ -205,11 +206,13 @@
     turn2 = turn2 - jnp.floor(turn2)
     first = c1 * (corner(own_boxes, 0)[0].astype(F32) + offs)
     first = first * first
+    block = delta_ref[boxes[0] : boxes[-1] + 1].reshape(len(boxes) * 2 * R, twice.shape[1])
+    picked = lax.dot_general(block, twice, CONTRACT, preferred_element_type=F32)
     sums = []
-    for b in boxes:
+    for n, b in enumerate(boxes):
         k1, k2 = corner(own_boxes, b)
-        picked = lax.dot_general(delta_ref[b], twice, CONTRACT, preferred_element_type=F32)
-        wr, wi = picked[:R], picked[R:]
+        at = 2 * R * n
+        wr, wi = picked[at : at + R], picked[at + R : at + 2 * R]
         whole = ((h1 * k1 + h2 * k2) & (GRID - 1)).astype(F32) * (1.0 / GRID)
         second = c2 * (k2.astype(F32) + offs)
         second = second * second

time: 34.4 us -> 32.5 us (0.945)
  Pallas kernels: 32.5 us -> 30.7 us
    pallas_call x1, Pallas kernels: 32.5 us -> 30.7 us  [local(): pl.pallas_call(lambda *refs: kernel(own_boxes, targets, parents, devices,...]
where the time goes in v3:
time: 32.5 us; the launch traced here: 32.3 us
  Pallas kernels  30.7 us (94%)
  local copies, waits for them, and re-layouts  1.67 us (5%)
    pallas_call x1, Pallas kernels, local(): pl.pallas_call(lambda *refs: kernel(own_boxes, targets, parents, devices,...  30.7 us
    unnamed x1, local copies, waits for them, and re-layouts  1.67 us

profile of v3, /device:TPU:0, one launch (start us, length us, event | category | flops | bytes accessed | tf_op | source)
XLA Modules:
  0.0 32.3 jit_solution(15979482250386182323)
XLA Ops:
  0.0 30.7 %shard_map.73 = f32[2,32,8,64]{3,2,1,0:T(8,128)} custom-call(f32[2,8,4,64,64]{4,3,2,1,0:T(8,128)} %refs_0_.1, s32[8,32]{1,0:T(8,128)} %refs_1_.1, s32[1,256]{1,0:T(1,128)} %bitcast.2, s32[1,256]{1,0:T(1,128)} %bitcast.3, bf16[128,256]{1,0:T(8,128)(2,1)} %constant.6.clone.refs_4_, f32[56,256]{1,0:T(8,128)} %constant.7.clone.refs_5_, ...), custom_call_target="tpu_custom_call" | custom-call | tf_op jit(solution)/shard_map/pallas_call | solution.py:451
  30.7 1.7 %copy.9 = f32[2,32,8,64]{3,2,1,0:T(8,128)} copy(f32[2,32,8,64]{3,2,1,0:T(8,128)} %shard_map.73) | data formatting | bytes 262144

commit v4 on v3

--- a/solution.py
+++ b/solution.py
@@ -304,10 +304,10 @@
         source_box(own_boxes, targets, parents, b, weights, table, centre, offset, delta)
         return carry
 
-    lax.fori_loop(0, 2, one_box, 0)
+    lax.fori_loop(0, 2, one_box, 0, unroll=2)
     pl.semaphore_wait(barrier, devices - 1)
     lax.fori_loop(1, devices, send_pivots, 0)
-    lax.fori_loop(2, own_boxes, one_box, 0)
+    lax.fori_loop(2, own_boxes, one_box, 0, unroll=2)
 
     boxes = LANES // RT
     groups = targets // devices // boxes
@@ -405,7 +405,7 @@
             rows_copy(half, lax.rem(me + j, devices), me).start()
             return carry
 
-        lax.fori_loop(0, spans, one_span, 0)
+        lax.fori_loop(0, spans, one_span, 0, unroll=2)
         lax.fori_loop(0, devices, place_rows, 0, unroll=8)
         lax.fori_loop(1, devices, send_rows, 0)
         got[half, me] = rows[half, me]

time: 32.5 us -> 32 us (0.985)
  Pallas kernels: 30.7 us -> 30.2 us
    pallas_call x1, Pallas kernels: 30.7 us -> 30.2 us  [local(): pl.pallas_call(lambda *refs: kernel(own_boxes, targets, parents, devices,...]
where the time goes in v4:
time: 32 us; the launch traced here: 31.8 us
  Pallas kernels  30.2 us (94%)
  local copies, waits for them, and re-layouts  1.67 us (5%)
    pallas_call x1, Pallas kernels, local(): pl.pallas_call(lambda *refs: kernel(own_boxes, targets, parents, devices,...  30.2 us
    unnamed x1, local copies, waits for them, and re-layouts  1.67 us

profile of v4, /device:TPU:0, one launch (start us, length us, event | category | flops | bytes accessed | tf_op | source)
XLA Modules:
  0.0 31.8 jit_solution(1181470782114900312)
XLA Ops:
  0.0 30.2 %shard_map.73 = f32[2,32,8,64]{3,2,1,0:T(8,128)} custom-call(f32[2,8,4,64,64]{4,3,2,1,0:T(8,128)} %refs_0_.1, s32[8,32]{1,0:T(8,128)} %refs_1_.1, s32[1,256]{1,0:T(1,128)} %bitcast.2, s32[1,256]{1,0:T(1,128)} %bitcast.3, bf16[128,256]{1,0:T(8,128)(2,1)} %constant.6.clone.refs_4_, f32[56,256]{1,0:T(8,128)} %constant.7.clone.refs_5_, ...), custom_call_target="tpu_custom_call" | custom-call | tf_op jit(solution)/shard_map/pallas_call | solution.py:451
  30.2 1.7 %copy.9 = f32[2,32,8,64]{3,2,1,0:T(8,128)} copy(f32[2,32,8,64]{3,2,1,0:T(8,128)} %shard_map.73) | data formatting | bytes 262144

commit v5 on v4

--- a/solution.py
+++ b/solution.py
@@ -267,7 +267,7 @@
     ]
     for copy in consts + loads:
         copy.start()
-    lax.fori_loop(1, devices, greet, 0)
+    lax.fori_loop(1, devices, greet, 0, unroll=True)
     for copy in consts:
         copy.wait()
 
@@ -306,7 +306,7 @@
 
     lax.fori_loop(0, 2, one_box, 0, unroll=2)
     pl.semaphore_wait(barrier, devices - 1)
-    lax.fori_loop(1, devices, send_pivots, 0)
+    lax.fori_loop(1, devices, send_pivots, 0, unroll=True)
     lax.fori_loop(2, own_boxes, one_box, 0, unroll=2)
 
     boxes = LANES // RT
@@ -407,7 +407,7 @@
 
         lax.fori_loop(0, spans, one_span, 0, unroll=2)
         lax.fori_loop(0, devices, place_rows, 0, unroll=8)
-        lax.fori_loop(1, devices, send_rows, 0)
+        lax.fori_loop(1, devices, send_rows, 0, unroll=True)
         got[half, me] = rows[half, me]
 
     drain(got.at[:, others], rows_send, rows_recv)

time: 32 us -> 31.8 us (level)
  no operation moved by 1% of the time
where the time goes in v5:
time: 31.8 us; the launch traced here: 31.6 us
  Pallas kernels  29.9 us (94%)
  local copies, waits for them, and re-layouts  1.67 us (5%)
    pallas_call x1, Pallas kernels, local(): pl.pallas_call(lambda *refs: kernel(own_boxes, targets, parents, devices,...  29.9 us
    unnamed x1, local copies, waits for them, and re-layouts  1.67 us

profile of v5, /device:TPU:0, one launch (start us, length us, event | category | flops | bytes accessed | tf_op | source)
XLA Modules:
  0.0 31.6 jit_solution(15078559659739527939)
XLA Ops:
  0.0 29.9 %shard_map.73 = f32[2,32,8,64]{3,2,1,0:T(8,128)} custom-call(f32[2,8,4,64,64]{4,3,2,1,0:T(8,128)} %refs_0_.1, s32[8,32]{1,0:T(8,128)} %refs_1_.1, s32[1,256]{1,0:T(1,128)} %bitcast.2, s32[1,256]{1,0:T(1,128)} %bitcast.3, bf16[128,256]{1,0:T(8,128)(2,1)} %constant.6.clone.refs_4_, f32[56,256]{1,0:T(8,128)} %constant.7.clone.refs_5_, ...), custom_call_target="tpu_custom_call" | custom-call | tf_op jit(solution)/shard_map/pallas_call | solution.py:451
  29.9 1.7 %copy.9 = f32[2,32,8,64]{3,2,1,0:T(8,128)} copy(f32[2,32,8,64]{3,2,1,0:T(8,128)} %shard_map.73) | data formatting | bytes 262144
